TPU v7x, 128 devices: a whole 4x4x4 slice. The times are simulated.
128 devices in a mesh: tm: 8 (over x, z_hi), clip: 16 (over z_lo, y, core).
Axes of the slice: x: 4, y: 4, z: 4 (z_hi: 2, z_lo: 2; z = z_hi * 2 + z_lo), core: 2. Of those that a mesh axis runs over, the one named last changes fastest.
Arguments:
- frame_tokens: bfloat16 [64, 8, 256, 512], P('clip', 'tm'), may hold values from -6 to 6
- actions: int32 [64, 8], P('clip', 'tm'), may hold values from 0 to 7
- frame_counts: int32 [64], P('clip'), may hold values from 2 to 8, as said below
- action_table: bfloat16 [8, 512], replicated, may hold values from -6 to 6
- ln_gain: float32 [3, 512], replicated, may hold values from 0.5 to 1.5
- ln_bias: float32 [3, 512], replicated, may hold values from -1.2 to 1.2
- w_sqkv: bfloat16 [512, 1536], replicated, may hold values from -0.25 to 0.25
- w_so: bfloat16 [512, 512], replicated, may hold values from -2 to 2
- w_tqkv: bfloat16 [512, 1536], replicated, may hold values from -0.25 to 0.25
- w_to: bfloat16 [512, 512], replicated, may hold values from -0.375 to 0.375
- w_up: bfloat16 [512, 2048], replicated, may hold values from -0.25 to 0.25
- b_up: float32 [2048], replicated, may hold values from -3 to 3
- w_down: bfloat16 [2048, 512], replicated, may hold values from -0.125 to 0.125
- cotangent: bfloat16 [64, 8, 256, 512], P('clip', 'tm'), may hold values from -6 to 6
Outputs:
- block_out: bfloat16 [64, 8, 256, 512], P('clip', 'tm')
- grad_input: float32 [64, 8, 256, 512], P('clip', 'tm')
- grad_table: float32 [8, 512], replicated
- grad_gain: float32 [3, 512], replicated
- grad_bias: float32 [3, 512], replicated
- grad_sqkv: float32 [512, 1536], replicated
- grad_so: float32 [512, 512], replicated
- grad_tqkv: float32 [512, 1536], replicated
- grad_to: float32 [512, 512], replicated
- grad_up: float32 [512, 2048], replicated
- up_bias_gradient: float32 [2048], replicated
- grad_down: float32 [2048, 512], replicated
Inputs may be any that keep to these rules, and one draw needn't show every extreme that they name: `frame_counts`: frames present in a clip come first in it; in each aligned block of 4 clips one clip holds all 8 frames.
All inputs are finite; a program needn't handle non-finite values.
Results may differ from a plain program's by a relative error of at most 0.014.
Values may be sent and summed in bfloat16 or wider, within the bound.
No kernel may reach another device: no remote copies, remote signals or barrier semaphores. Data moves between devices by JAX's collectives and lax.ppermute only.
A program may use at most 256 MiB of HBM per device.

v0:
```python
import math

import jax
import jax.numpy as jnp
from jax import lax
from jax.sharding import PartitionSpec as P

HEADS = 8


eps_norm = 1e-05
big_negative = -1e30


def layer_norm(values, gain_row, shift_row):
    center = values - jnp.mean(values, axis=-1, keepdims=True)
    spread = jnp.mean(center * center, axis=-1, keepdims=True)
    return center * lax.rsqrt(spread + eps_norm) * gain_row + shift_row


def norm_back(values, gain_row, shift_row, upstream):
    _, pull = jax.vjp(layer_norm, values, gain_row, shift_row)
    return pull(upstream)


def right_mul(values, weight):
    return jnp.dot(values, weight, preferred_element_type=jnp.float32)


def backward_multiply(values, weight):
    return lax.dot_general(
        values, weight, (((values.ndim - 1,), (1,)), ((), ())), preferred_element_type=jnp.float32
    )


def weight_gradient(left_side, right_side):
    left_flat = left_side.reshape(-1, left_side.shape[-1])
    right_flat = right_side.reshape(-1, right_side.shape[-1])
    return lax.dot_general(
        left_flat, right_flat, (((0,), (0,)), ((), ())), preferred_element_type=jnp.float32
    )


def shards(
    frame_tokens,
    actions,
    frame_counts,
    action_table,
    ln_gain,
    ln_bias,
    w_sqkv,
    w_so,
    w_tqkv,
    w_to,
    w_up,
    b_up,
    w_down,
    cotangent,
):
    clip_count, frames_here, patch_len, model_width = frame_tokens.shape
    head_count = HEADS
    head_dim = model_width // head_count
    score_scale = 1.0 / math.sqrt(head_dim)
    frame_rows = clip_count * frames_here
    frames_all = frames_here * lax.axis_size("tm")
    frame_ids = lax.axis_index("tm") * frames_here + jnp.arange(frames_here, dtype=jnp.int32)
    key_ids = jnp.arange(frames_all, dtype=jnp.int32)
    frame_mask = (frame_ids[None, :] < frame_counts[:, None]).astype(jnp.float32)
    allowed = (key_ids[None, None, :] < frame_counts[:, None, None]) & (
        key_ids[None, None, :] <= frame_ids[None, :, None]
    )
    allowed = allowed[:, None, None, :, :]
    onehot = (actions[..., None] == jnp.arange(action_table.shape[0], dtype=jnp.int32)).astype(
        jnp.float32
    )
    embedded = jnp.einsum(
        "cfa,ad->cfd", onehot, action_table.astype(jnp.float32), precision=lax.Precision.HIGHEST
    )
    first_state = frame_tokens.astype(jnp.float32) + embedded[:, :, None, :]
    act_one = layer_norm(first_state, ln_gain[0], ln_bias[0]).astype(jnp.bfloat16)
    s_qkv = (
        right_mul(act_one, w_sqkv)
        .astype(jnp.bfloat16)
        .reshape(frame_rows, patch_len, 3, head_count, head_dim)
    )
    s_query, s_key, s_value = (s_qkv[:, :, 0], s_qkv[:, :, 1], s_qkv[:, :, 2])
    s_scores = (
        jnp.einsum("nphd,nqhd->nhpq", s_query, s_key, preferred_element_type=jnp.float32)
        * score_scale
    )
    s_probs = jax.nn.softmax(s_scores, axis=-1)
    s_low = s_probs.astype(jnp.bfloat16)
    s_out = jnp.einsum(
        "nhpq,nqhd->nphd", s_low, s_value, preferred_element_type=jnp.float32
    ).astype(jnp.bfloat16)
    s_out = s_out.reshape(clip_count, frames_here, patch_len, model_width)
    mid_state = first_state + right_mul(s_out, w_so)
    act_two = layer_norm(mid_state, ln_gain[1], ln_bias[1]).astype(jnp.bfloat16)
    t_qkv = right_mul(act_two, w_tqkv).astype(jnp.bfloat16)
    t_query = t_qkv[..., :model_width].reshape(
        clip_count, frames_here, patch_len, head_count, head_dim
    )
    kv_local = t_qkv[..., model_width:]
    whole = lax.all_gather(kv_local, "tm", axis=1, tiled=True)
    frame_total = whole.shape[1]
    key_part = whole[..., :model_width].reshape(
        clip_count, frame_total, patch_len, head_count, head_dim
    )
    value_part = whole[..., model_width:].reshape(
        clip_count, frame_total, patch_len, head_count, head_dim
    )
    t_scores = (
        jnp.einsum("cfphd,cephd->cphfe", t_query, key_part, preferred_element_type=jnp.float32)
        * score_scale
    )
    t_scores = jnp.where(allowed, t_scores, big_negative)
    t_probs = jax.nn.softmax(t_scores, axis=-1)
    t_low = t_probs.astype(jnp.bfloat16)
    t_out = jnp.einsum(
        "cphfe,cephd->cfphd", t_low, value_part, preferred_element_type=jnp.float32
    ).astype(jnp.bfloat16)
    t_out = t_out.reshape(clip_count, frames_here, patch_len, model_width)
    late_state = mid_state + right_mul(t_out, w_to)
    act_three = layer_norm(late_state, ln_gain[2], ln_bias[2]).astype(jnp.bfloat16)
    pre_act = right_mul(act_three, w_up) + b_up
    hidden = jax.nn.gelu(pre_act).astype(jnp.bfloat16)
    block_out = (late_state + right_mul(hidden, w_down)).astype(jnp.bfloat16)
    d_out = cotangent.astype(jnp.float32) * frame_mask[:, :, None, None]
    d_down = d_out.astype(jnp.bfloat16)
    grad_down = weight_gradient(hidden, d_down)
    d_hidden = backward_multiply(d_down, w_down)
    _, gelu_pull = jax.vjp(jax.nn.gelu, pre_act)
    d_pre = gelu_pull(d_hidden)[0].astype(jnp.bfloat16)
    grad_up = weight_gradient(act_three, d_pre)
    up_bias_gradient = jnp.sum(d_pre.astype(jnp.float32), axis=(0, 1, 2))
    d_norm3, gain_three, bias_three = norm_back(
        late_state, ln_gain[2], ln_bias[2], backward_multiply(d_pre, w_up)
    )
    d_late = d_out + d_norm3
    ffn_part = (grad_up, up_bias_gradient, grad_down, gain_three, bias_three)
    d_tproj = d_late.astype(jnp.bfloat16)
    grad_to = weight_gradient(t_out, d_tproj)
    d_tout = (
        backward_multiply(d_tproj, w_to)
        .astype(jnp.bfloat16)
        .reshape(clip_count, frames_here, patch_len, head_count, head_dim)
    )
    d_tprob = jnp.einsum(
        "cfphd,cephd->cphfe", d_tout, value_part, preferred_element_type=jnp.float32
    )
    t_delta = jnp.sum(t_probs * d_tprob, axis=-1, keepdims=True)
    d_tscore = (t_probs * (d_tprob - t_delta)).astype(jnp.bfloat16)
    d_tquery = (
        jnp.einsum("cphfe,cephd->cfphd", d_tscore, key_part, preferred_element_type=jnp.float32)
        * score_scale
    )
    row_count = frames_here * lax.axis_size("tm")
    d_key = (
        jnp.einsum("cphfe,cfphd->ecphd", d_tscore, t_query, preferred_element_type=jnp.float32)
        * score_scale
    )
    d_value = jnp.einsum("cphfe,cfphd->ecphd", t_low, d_tout, preferred_element_type=jnp.float32)
    d_kv = lax.psum_scatter(
        jnp.concatenate(
            [
                d_key.reshape(row_count, clip_count, patch_len, model_width),
                d_value.reshape(row_count, clip_count, patch_len, model_width),
            ],
            axis=-1,
        ).astype(jnp.bfloat16),
        "tm",
        scatter_dimension=0,
        tiled=True,
    ).astype(jnp.float32)
    d_kv = jnp.transpose(d_kv, (1, 0, 2, 3))
    d_tqkv = jnp.concatenate(
        [d_tquery.reshape(clip_count, frames_here, patch_len, model_width), d_kv], axis=-1
    ).astype(jnp.bfloat16)
    grad_tqkv = weight_gradient(act_two, d_tqkv)
    d_norm2, gain_two, bias_two = norm_back(
        mid_state, ln_gain[1], ln_bias[1], backward_multiply(d_tqkv, w_tqkv)
    )
    d_mid = d_late + d_norm2
    temporal_part = (grad_tqkv, grad_to, gain_two, bias_two)
    d_sproj = d_mid.astype(jnp.bfloat16)
    grad_so = weight_gradient(s_out, d_sproj)
    d_sout = (
        backward_multiply(d_sproj, w_so)
        .astype(jnp.bfloat16)
        .reshape(frame_rows, patch_len, head_count, head_dim)
    )
    d_sprob = jnp.einsum("nphd,nqhd->nhpq", d_sout, s_value, preferred_element_type=jnp.float32)
    s_delta = jnp.sum(s_probs * d_sprob, axis=-1, keepdims=True)
    d_sscore = (s_probs * (d_sprob - s_delta)).astype(jnp.bfloat16)
    spatial_query_gradient = (
        jnp.einsum("nhpq,nqhd->nphd", d_sscore, s_key, preferred_element_type=jnp.float32)
        * score_scale
    )
    spatial_key_gradient = (
        jnp.einsum("nhpq,nphd->nqhd", d_sscore, s_query, preferred_element_type=jnp.float32)
        * score_scale
    )
    spatial_value_gradient = jnp.einsum(
        "nhpq,nphd->nqhd", s_low, d_sout, preferred_element_type=jnp.float32
    )
    spatial_projection_gradient = jnp.stack(
        [spatial_query_gradient, spatial_key_gradient, spatial_value_gradient], axis=2
    ).reshape(clip_count, frames_here, patch_len, 3 * model_width)
    spatial_projection_gradient = spatial_projection_gradient.astype(jnp.bfloat16)
    grad_sqkv = weight_gradient(act_one, spatial_projection_gradient)
    d_norm1, gain_one, bias_one = norm_back(
        first_state, ln_gain[0], ln_bias[0], backward_multiply(spatial_projection_gradient, w_sqkv)
    )
    grad_input = d_mid + d_norm1
    frame_sums = jnp.sum(grad_input, axis=2)
    grad_table = jnp.einsum("cfa,cfd->ad", onehot, frame_sums, precision=lax.Precision.HIGHEST)
    spatial_part = (grad_sqkv, grad_so, gain_one, bias_one, grad_table)
    summed = ffn_part + temporal_part + spatial_part
    summed = lax.psum(summed, ("tm", "clip"))
    (
        grad_up,
        up_bias_gradient,
        grad_down,
        gain_three,
        bias_three,
        grad_tqkv,
        grad_to,
        gain_two,
        bias_two,
        grad_sqkv,
        grad_so,
        gain_one,
        bias_one,
        grad_table,
    ) = summed
    grad_gain = jnp.stack([gain_one, gain_two, gain_three], axis=0)
    grad_bias = jnp.stack([bias_one, bias_two, bias_three], axis=0)
    return (
        block_out,
        grad_input,
        grad_table,
        grad_gain,
        grad_bias,
        grad_sqkv,
        grad_so,
        grad_tqkv,
        grad_to,
        grad_up,
        up_bias_gradient,
        grad_down,
    )


def solution(mesh):
    in_specs = (
        P("clip", "tm", None, None),
        P("clip", "tm"),
        P("clip"),
        P(),
        P(),
        P(),
        P(),
        P(),
        P(),
        P(),
        P(),
        P(),
        P(),
        P("clip", "tm", None, None),
    )
    out_specs = (
        P("clip", "tm", None, None),
        P("clip", "tm", None, None),
        P(),
        P(),
        P(),
        P(),
        P(),
        P(),
        P(),
        P(),
        P(),
        P(),
    )
    return jax.shard_map(shards, mesh=mesh, in_specs=in_specs, out_specs=out_specs, check_vma=False)
```

profile of v0, /device:TPU:1, one launch (start us, length us, event | category | flops | bytes accessed | tf_op | source)
XLA Modules:
  0.0 842.0 jit_solution(15253249235514504297)
XLA Ops:
  14.3 5.0 convolution_convert_fusion.1
  19.4 4.6 copy.76
  24.0 2.8 fusion.63
  26.8 6.3 fusion.101
  33.2 3.0 fusion.47
  39.6 1.9 fusion.12
  45.1 2.3 slice.60
  51.0 182.7 %all-gather.2.cloned.1.call-done = bf16[4,8,256,1024]{3,2,0,1:T(8,128)(2,1)} async-done(((bf16[4,1,256,1024]{3,2,0,1:T(8,128)(2,1)}), bf16[4,8,256,1024]{3,2,0,1:T(8,128)(2,1)}) %all-gather.2.cloned.1.call-update) | async-done | bytes 16777232 | tf_op jit(solution)/shard_map/all_gather | solution.py:104
  233.7 11.5 %fusion.98 = (bf16[4,8,256,512]{3,2,0,1:T(8,128)(2,1)}, bf16[4,8,256,512]{3,2,0,1:T(8,128)(2,1)}) fusion(bf16[4,8,256,1024]{3,2,0,1:T(8,128)(2,1)} %all-gather.2.cloned.1.call-done), kind=kLoop, calls=%fused_computation.157 | loop fusion | bytes 33554432 | tf_op jit(solution)/shard_map/slice | solution.py:106
  245.2 11.4 %copy.148 = bf16[4,8,256,512]{2,3,1,0:T(8,128)(2,1)} copy(bf16[4,8,256,512]{3,2,0,1:T(8,128)(2,1)} %get-tuple-element.72) | data formatting | bytes 16777216
  256.6 7.4 multiply_reduce_fusion.3
  265.1 11.4 %copy.147 = bf16[4,8,256,512]{2,3,1,0:T(8,128)(2,1)} copy(bf16[4,8,256,512]{3,2,0,1:T(8,128)(2,1)} %get-tuple-element.73) | data formatting | bytes 16777216
  276.4 6.0 multiply_reduce_fusion.2
  283.7 1.9 copy-done.55
  285.6 2.5 fusion.28
  288.2 8.0 convert_reduce_fusion
  296.2 3.3 fusion.13
  304.8 2.7 copy.87
  309.0 7.6 multiply_reduce_fusion.1
  316.9 5.6 multiply_convert_fusion.1
  322.6 12.2 %copy.88 = bf16[8,4,256,512]{3,2,1,0:T(8,128)(2,1)} copy(bf16[8,4,256,512]{2,3,1,0:T(8,128)(2,1)} %bitcast.271) | data formatting | bytes 16777216 | tf_op jit(solution)/shard_map/reshape | solution.py:166
  334.8 8.7 %multiply_convert_fusion = bf16[4,256,8,64,8]{1,3,2,0,4:T(8,128)(2,1)} fusion(f32[4,256,8,8]{1,2,0,3:T(8,128)S(1)} %copy-done.35, f32[4,256,8,64]{1,3,2,0:T(8,128)} %copy-done.13), kind=kLoop, calls=%fused_computation.6 | loop fusion | flops 8388608 | bytes 10747904 | tf_op jit(solution)/shard_map/convert.11
  343.4 12.1 %copy.89 = bf16[8,4,256,512]{3,2,1,0:T(8,128)(2,1)} copy(bf16[8,4,256,512]{2,3,1,0:T(8,128)(2,1)} %bitcast.270) | data formatting | bytes 16777216 | tf_op jit(solution)/shard_map/reshape | solution.py:167
  355.6 14.0 %pad_maximum_fusion = bf16[8,4,256,1024]{3,2,1,0:T(8,128)(2,1)} fusion(bf16[8,4,256,512]{3,2,1,0:T(8,128)(2,1)} %copy.89, bf16[8,4,256,512]{3,2,1,0:T(8,128)(2,1)} %copy.88), kind=kLoop, calls=%fused_computation.1 | loop fusion | flops 33554432 | bytes 33554432 | tf_op jit(solution)/shard_map/concatenate | solution.py:164
  369.8 2.0 copy.99
  375.0 6.8 multiply_reduce_fusion
  383.4 3.4 fusion.105
  386.8 6.9 convolution_bitcast_fusion.3
  393.8 9.9 %convolution_bitcast_fusion.2 = f32[2048,512]{1,0:T(8,128)} fusion(bf16[4,1,256,512]{3,2,1,0:T(8,128)(2,1)S(1)} %copy-done.21, f32[4]{0:T(128)S(1)} %copy-done.48, f32[4,256,2048]{2,1,0:T(8,128)} %copy-done.63, f32[2048]{0:T(1024)S(1)} %copy-done.61), kind=kOutput, calls=%fused_computation.32 | convolution fusion | flops 2170028032 | bytes 13639696 | tf_op jit(solution)/shard_map/dot_general | solution.py:39
  403.6 154.7 %reduce-scatter.2.cloned.1.call-done = bf16[1,4,256,1024]{3,2,1,0:T(8,128)(2,1)} async-done(((bf16[8,4,256,1024]{3,2,1,0:T(8,128)(2,1)}), bf16[1,4,256,1024]{3,2,1,0:T(8,128)(2,1)}) %reduce-scatter.2.cloned.1.call-update) | async-done | bytes 2097168 | tf_op jit(solution)/shard_map/reduce_scatter | solution.py:163
  558.3 5.1 fusion.17
  563.5 3.7 convolution_bitcast_fusion
  568.8 2.0 fusion.96
  575.3 4.9 fusion.39
  580.2 4.4 multiply_reduce_fusion.4
  590.6 3.8 convolution_bitcast_fusion.1
  596.1 1.8 reduce_sum.247
  597.9 8.1 fusion.52
  606.0 2.4 reduce_sum.246
  608.4 5.8 fusion.16
  614.2 1.8 reduce_sum.245
  616.0 2.8 fusion.95
  618.9 3.7 fusion.15
  622.9 68.0 %all-reduce = (f32[8,512]{1,0:T(8,128)}, f32[1,512]{1,0:T(1,128)S(1)}, f32[1,512]{1,0:T(1,128)S(1)}, f32[1,512]{1,0:T(1,128)S(1)}, f32[1,512]{1,0:T(1,128)S(1)},...) all-reduce(f32[8,512]{1,0:T(8,128)S(1)} %fusion.88, ...), channel_id=1, replica_groups=mesh['tm'=8,'clip'=16] {'tm','clip'}, use_global_device_ids=true, to_apply=%region_20.21 | all-reduce | flops 9216 | bytes 73728 | tf_op jit(solution)/shard_map/psum | solution.py:219
  691.5 128.9 %all-reduce.4.cloned.1.call-done = (f32[512,1536]{1,0:T(8,128)}, f32[512,512]{1,0:T(8,128)}, f32[512,1536]{1,0:T(8,128)}, f32[512,512]{1,0:T(8,128)}, f32[512,2048]{1,0:T(8,128)}, /*index=5*/f32[2048,512]{1,0:T(8,128)}) async-done(((f32[512,1536]{1,0:T(8,128)}, f32[512,512]{1,0:T(8,128)}, f32[512,1536]{1,0:T(8,128)}, f32[512,512]{1,0:T(8,128)}, f32[512,2048]{1,0:T(8,128)}, ...) | async-done | bytes 16777232 | tf_op jit(solution)/shard_map/psum | solution.py:219
  820.4 3.9 copy.188
  829.3 2.1 copy.192
  833.0 2.0 copy.193
  (193 shorter events, 53.2 us)
Async XLA Ops:
  7.2 280.9 %copy-start = (bf16[2048,512]{1,0:T(8,128)(2,1)S(1)}, bf16[2048,512]{1,0:T(8,128)(2,1)}, u32[]{:S(2)}) copy-start(bf16[2048,512]{1,0:T(8,128)(2,1)} %param.26) | copy-start | bytes 6291460
  7.2 7.2 copy-start.14
  7.2 226.5 %all-gather.2.cloned.1.call-start = ((), (), s32[]{:S(2)}) async-start(), calls=%async_computation.1 | async-start | bytes 18874368 | tf_op jit(solution)/shard_map/all_gather | solution.py:104
  8.2 11.2 %copy-start.45 = (f32[1,512]{1,0:T(1,128)}, f32[1,512]{1,0:T(1,128)S(1)}, u32[]{:S(2)}) copy-start(f32[1,512]{1,0:T(1,128)S(1)} %get-tuple-element.76) | copy-start | bytes 6148
  9.0 10.4 %copy-start.50 = (f32[1,512]{1,0:T(1,128)}, f32[1,512]{1,0:T(1,128)S(1)}, u32[]{:S(2)}) copy-start(f32[1,512]{1,0:T(1,128)S(1)} %get-tuple-element.79) | copy-start | bytes 6148
  9.0 28.9 %copy-start.52 = (f32[1,512]{1,0:T(1,128)}, f32[1,512]{1,0:T(1,128)S(1)}, u32[]{:S(2)}) copy-start(f32[1,512]{1,0:T(1,128)S(1)} %get-tuple-element.80) | copy-start | bytes 6148
  9.9 26.6 %copy-start.37 = (f32[4,512]{1,0:T(4,128)}, f32[4,512]{1,0:T(4,128)S(1)}, u32[]{:S(2)}) copy-start(f32[4,512]{1,0:T(4,128)S(1)} %fusion.89) | copy-start | bytes 24580
  33.1 3.4 copy-start.1
  33.1 3.3 copy-start.58
  37.5 4.1 copy-start.2
  44.8 513.5 %reduce-scatter.2.cloned.1.call-start = ((), (), s32[]{:S(2)}) async-start(), calls=%async_computation.2 | async-start | bytes 18874368 | tf_op jit(solution)/shard_map/reduce_scatter | solution.py:163
  276.4 6.0 copy-start.3
  276.4 6.0 copy-start.36
  283.3 16.2 %copy-start.5 = (f32[4,1,256,512]{3,2,0,1:T(8,128)}, f32[4,1,256,512]{3,2,0,1:T(8,128)S(1)}, u32[]{:S(2)}) copy-start(f32[4,1,256,512]{3,2,0,1:T(8,128)S(1)} %get-tuple-element.86) | copy-start | bytes 6291460
  283.3 2.4 copy-start.55
  285.6 2.5 copy-start.20
  285.6 2.5 copy-start.47
  285.6 2.5 copy-start.60
  288.1 8.0 copy-start.63
  296.2 3.3 copy-start.19
  309.0 7.6 copy-start.13
  309.0 7.9 copy-start.12
  316.9 5.7 copy-start.25
  322.6 12.2 %copy-start.35 = (f32[4,256,8,8]{1,2,0,3:T(8,128)S(1)}, f32[4,256,8,8]{1,2,0,3:T(8,128)}, u32[]{:S(2)}) copy-start(f32[4,256,8,8]{1,2,0,3:T(8,128)} %convert_convert_fusion) | copy-start | bytes 786436
  369.6 450.8 %all-reduce.4.cloned.1.call-start = ((), (), s32[]{:S(2)}) async-start(), calls=%async_computation.3 | async-start | bytes 33554432 | tf_op jit(solution)/shard_map/psum | solution.py:219
  383.4 3.4 copy-start.6
  386.8 6.9 copy-start.21
  386.8 6.9 copy-start.48
  386.8 6.9 copy-start.61
  558.3 5.1 copy-start.4
  558.3 5.1 copy-start.32
  558.3 5.1 copy-start.53
  558.3 5.1 copy-start.56
  563.5 4.9 copy-start.10
  568.8 3.0 copy-start.59
  575.2 5.0 copy-start.7
  575.2 9.4 %slice-start = ((s8[8388608]{0:T(1024)(128)(4,1)}), s8[4194304]{0:T(1024)(128)(4,1)S(1)}, s32[]{:S(2)}) async-start(s8[8388608]{0:T(1024)(128)(4,1)} %bitcast.268), calls=%async_computation.4 | async-start | bytes 8388608
  580.2 4.8 slice-start.1
  589.8 4.6 copy-start.23
  590.6 3.9 copy-start.31
  590.6 3.9 copy-start.34
  616.0 2.9 copy-start.11
  618.9 3.7 copy-start.62
  618.9 3.9 copy-start.49
  820.4 3.9 copy-start.30
  820.4 4.9 copy-start.22
  825.3 4.0 copy-start.18
  829.3 3.7 copy-start.17
  (21 other events, 29.1 us)
Sparse Core Ops, SparseCore 0:
  44.9 188.7 all-gather.1
  369.7 188.5 reduce-scatter.1
  596.3 224.0 all-reduce.3
where the time goes:
time: 850 us; the launch traced here: 842 us
  waiting for transfers between devices  466 us (55%)
  local copies, waits for them, and re-layouts  108 us (13%)
  matrix products  92.8 us (11%)
  other arithmetic  91.3 us (11%)
  blocking collectives  68 us (8%)
  between operations  14.9 us (2%)
    all_gather x1, waiting for transfers between devices, shards(): whole = lax.all_gather(kv_local, 'tm', axis=1, tiled=True)  183 us
    reduce_scatter x1, waiting for transfers between devices, shards(): lax.psum_scatter(jnp.concatenate([d_key.reshape(row_count, clip_count, pa...  155 us
    psum x1, waiting for transfers between devices, shards(): summed = lax.psum(summed, ('tm', 'clip'))  129 us
    psum x1, blocking collectives, shards(): summed = lax.psum(summed, ('tm', 'clip'))  68 us
    unnamed x142, local copies, waits for them, and re-layouts  51.7 us
    dot_general x6, matrix products, weight_gradient(): lax.dot_general(left_flat, right_flat, (((0,), (0,)), ((), ())), preferre...  29.4 us
    dot_general x6, matrix products, backward_multiply(): lax.dot_general(values, weight, (((values.ndim - 1,), (1,)), ((), ())), p...  25.7 us
    dot_general x6, matrix products, right_mul(): return jnp.dot(values, weight, preferred_element_type=jnp.float32)  19.1 us
  transfers between devices with their start and end apart: 3, of which 3 were waited for; matrix products, arithmetic and copies ran while one was open for 8% of the time, Pallas kernels for 0%

commit v1 on v0

v1 whole, which is shorter than its diff:
```python
import math

import jax
import jax.numpy as jnp
from jax import lax
from jax.sharding import Mesh, PartitionSpec as P

HEADS = 8
EPS = 1e-05
NEG = -1e30
BF = jnp.bfloat16
F32 = jnp.float32
FRAME_AXES = ("x", "zh")
CHIP_AXES = ("x", "zh", "zl", "y")


def layer_norm(values, gain_row, shift_row):
    center = values - jnp.mean(values, axis=-1, keepdims=True)
    spread = jnp.mean(center * center, axis=-1, keepdims=True)
    return center * lax.rsqrt(spread + EPS) * gain_row + shift_row


def norm_back(values, gain_row, shift_row, upstream):
    _, pull = jax.vjp(layer_norm, values, gain_row, shift_row)
    return pull(upstream)


def mul(a, b):
    return jnp.dot(a, b, preferred_element_type=F32)


def mul_t(a, b):
    return lax.dot_general(a, b, (((a.ndim - 1,), (1,)), ((), ())), preferred_element_type=F32)


def wgrad(a, b):
    a = a.reshape(-1, a.shape[-1])
    b = b.reshape(-1, b.shape[-1])
    return lax.dot_general(a, b, (((0,), (0,)), ((), ())), preferred_element_type=F32)


def to_positions(v):
    clips, patch, width = v.shape
    n = lax.axis_size(FRAME_AXES)
    v = v.reshape(clips, n, patch // n, width).transpose(1, 0, 2, 3)
    return lax.all_to_all(v, FRAME_AXES, 0, 0)


def to_frames(v):
    n, clips, part, width = v.shape
    v = lax.all_to_all(v, FRAME_AXES, 0, 0)
    return v.transpose(1, 0, 2, 3).reshape(clips, n * part, width)


def swap_cores(v):
    return lax.ppermute(v, "c", [(0, 1), (1, 0)])


def reduce_rows(v):
    rows, width = v.shape
    core = lax.axis_index("c")
    chips = lax.axis_size(CHIP_AXES)
    halves = v.reshape(2, rows // 2, width)
    mine = lax.dynamic_index_in_dim(halves, core, 0, keepdims=False)
    other = lax.dynamic_index_in_dim(halves, 1 - core, 0, keepdims=False)
    got = swap_cores(other.astype(BF))
    half = (mine.astype(F32) + got.astype(F32)).astype(BF)
    parts = lax.all_to_all(half.reshape(chips, -1, width), CHIP_AXES, 0, 0)
    part = jnp.sum(parts.astype(F32), axis=0).astype(BF)
    whole = lax.all_to_all(jnp.broadcast_to(part[None], (chips, *part.shape)), CHIP_AXES, 0, 0)
    whole = whole.reshape(rows // 2, width)
    peer = swap_cores(whole)
    first = jnp.where(core == 0, whole, peer)
    second = jnp.where(core == 0, peer, whole)
    return jnp.concatenate([first, second], axis=0)


def shards(
    frame_tokens, actions, frame_counts, action_table, ln_gain, ln_bias, w_sqkv, w_so, w_tqkv, w_to,
    w_up, b_up, w_down, cotangent,
):
    clips, _, patch, width = frame_tokens.shape
    heads = HEADS
    dim = width // heads
    scale = 1.0 / math.sqrt(dim)
    cot = to_positions(cotangent[:, 0])
    frames, _, part, _ = cot.shape
    onehot = (actions[:, 0, None] == jnp.arange(action_table.shape[0], dtype=jnp.int32)).astype(F32)
    embedded = jnp.dot(onehot, action_table.astype(F32), precision=lax.Precision.HIGHEST)
    first_state = frame_tokens[:, 0].astype(F32) + embedded[:, None, :]
    act_one = layer_norm(first_state, ln_gain[0], ln_bias[0]).astype(BF)
    s_qkv = mul(act_one, w_sqkv).astype(BF).reshape(clips, patch, 3, heads, dim)
    s_query, s_key, s_value = s_qkv[:, :, 0], s_qkv[:, :, 1], s_qkv[:, :, 2]
    s_scores = jnp.einsum("nphd,nqhd->nhpq", s_query, s_key, preferred_element_type=F32) * scale
    s_probs = jax.nn.softmax(s_scores, axis=-1)
    s_low = s_probs.astype(BF)
    s_out = jnp.einsum("nhpq,nqhd->nphd", s_low, s_value, preferred_element_type=F32).astype(BF)
    s_out = s_out.reshape(clips, patch, width)
    mid_here = (first_state + mul(s_out, w_so)).astype(BF)

    mid_state = to_positions(mid_here).astype(F32)
    frame_ids = jnp.arange(frames, dtype=jnp.int32)
    mask = (frame_ids[:, None] < frame_counts[None, :]).astype(F32)[:, :, None, None]
    allowed = (frame_ids[None, None, :] < frame_counts[:, None, None]) & (
        frame_ids[None, None, :] <= frame_ids[None, :, None]
    )
    act_two = layer_norm(mid_state, ln_gain[1], ln_bias[1]).astype(BF)
    t_qkv = mul(act_two, w_tqkv).astype(BF).reshape(frames, clips, part, 3, heads, dim)
    t_query, t_key, t_value = t_qkv[..., 0, :, :], t_qkv[..., 1, :, :], t_qkv[..., 2, :, :]
    t_scores = jnp.einsum("fcphd,ecphd->cphfe", t_query, t_key, preferred_element_type=F32) * scale
    t_probs = jax.nn.softmax(jnp.where(allowed[:, None, None], t_scores, NEG), axis=-1)
    t_low = t_probs.astype(BF)
    t_out = jnp.einsum("cphfe,ecphd->fcphd", t_low, t_value, preferred_element_type=F32).astype(BF)
    t_out = t_out.reshape(frames, clips, part, width)
    late_state = mid_state + mul(t_out, w_to)
    act_three = layer_norm(late_state, ln_gain[2], ln_bias[2]).astype(BF)
    pre_act = mul(act_three, w_up) + b_up
    hidden, gelu_pull = jax.vjp(jax.nn.gelu, pre_act)
    hidden = hidden.astype(BF)
    block_out = to_frames((late_state + mul(hidden, w_down)).astype(BF))
    d_out = cot.astype(F32) * mask
    d_down = d_out.astype(BF)
    grad_down = wgrad(hidden, d_down)
    d_pre = gelu_pull(mul_t(d_down, w_down))[0].astype(BF)
    grad_up = wgrad(act_three, d_pre)
    up_bias = jnp.sum(d_pre.astype(F32), axis=(0, 1, 2))
    d_norm3, gain_three, bias_three = norm_back(late_state, ln_gain[2], ln_bias[2], mul_t(d_pre, w_up))
    d_late = d_out + d_norm3
    chunks = w_up.shape[1] // width
    ffn = reduce_rows(
        jnp.concatenate(
            [
                grad_up.astype(BF).reshape(width, chunks, width).transpose(1, 0, 2).reshape(-1, width),
                grad_down.astype(BF),
            ],
            axis=0,
        )
    )
    d_tproj = d_late.astype(BF)
    grad_to = wgrad(t_out, d_tproj)
    d_tout = mul_t(d_tproj, w_to).astype(BF).reshape(frames, clips, part, heads, dim)
    d_tprob = jnp.einsum("fcphd,ecphd->cphfe", d_tout, t_value, preferred_element_type=F32)
    t_delta = jnp.sum(t_probs * d_tprob, axis=-1, keepdims=True)
    d_tscore = (t_probs * (d_tprob - t_delta)).astype(BF)
    d_tq = jnp.einsum("cphfe,ecphd->fcphd", d_tscore, t_key, preferred_element_type=F32) * scale
    d_tk = jnp.einsum("cphfe,fcphd->ecphd", d_tscore, t_query, preferred_element_type=F32) * scale
    d_tv = jnp.einsum("cphfe,fcphd->ecphd", t_low, d_tout, preferred_element_type=F32)
    d_tqkv = jnp.concatenate(
        [v.reshape(frames, clips, part, width) for v in (d_tq, d_tk, d_tv)], axis=-1
    ).astype(BF)
    grad_tqkv = wgrad(act_two, d_tqkv)
    d_norm2, gain_two, bias_two = norm_back(mid_state, ln_gain[1], ln_bias[1], mul_t(d_tqkv, w_tqkv))
    d_mid = to_frames((d_late + d_norm2).astype(BF))

    grad_so = wgrad(s_out, d_mid)
    d_sout = mul_t(d_mid, w_so).astype(BF).reshape(clips, patch, heads, dim)
    d_sprob = jnp.einsum("nphd,nqhd->nhpq", d_sout, s_value, preferred_element_type=F32)
    s_delta = jnp.sum(s_probs * d_sprob, axis=-1, keepdims=True)
    d_sscore = (s_probs * (d_sprob - s_delta)).astype(BF)
    d_sq = jnp.einsum("nhpq,nqhd->nphd", d_sscore, s_key, preferred_element_type=F32) * scale
    d_sk = jnp.einsum("nhpq,nphd->nqhd", d_sscore, s_query, preferred_element_type=F32) * scale
    d_sv = jnp.einsum("nhpq,nphd->nqhd", s_low, d_sout, preferred_element_type=F32)
    d_sqkv = jnp.concatenate([v.reshape(clips, patch, width) for v in (d_sq, d_sk, d_sv)], axis=-1)
    d_sqkv = d_sqkv.astype(BF)
    grad_sqkv = wgrad(act_one, d_sqkv)
    d_norm1, gain_one, bias_one = norm_back(first_state, ln_gain[0], ln_bias[0], mul_t(d_sqkv, w_sqkv))
    grad_input = d_mid.astype(F32) + d_norm1
    frame_sums = jnp.sum(grad_input, axis=1)
    grad_table = jnp.einsum("ca,cd->ad", onehot, frame_sums, precision=lax.Precision.HIGHEST)

    def blocks(v):
        return v.reshape(width, -1, width).transpose(1, 0, 2).reshape(-1, width)

    small = jnp.concatenate(
        [
            grad_table,
            jnp.stack([gain_one, gain_two, gain_three, bias_one, bias_two, bias_three]),
            up_bias.reshape(-1, width),
        ],
        axis=0,
    )
    devices = lax.axis_size(CHIP_AXES) * lax.axis_size("c")
    per_device = small.size // devices
    main = jnp.concatenate([blocks(grad_tqkv), grad_to, blocks(grad_sqkv), grad_so], axis=0)
    rows = main.shape[0] // devices
    extra = jnp.pad(small.reshape(devices, 1, per_device), ((0, 0), (0, rows - 1), (0, 128 - per_device)))
    main = jnp.concatenate([main.reshape(devices, rows, width), extra], axis=-1)
    rest = reduce_rows(main.reshape(devices * rows, width + 128)).astype(F32)
    small = rest.reshape(devices, rows, width + 128)[:, 0, width : width + per_device].reshape(-1, width)
    main = rest[:, :width]

    def unblock(v):
        return v.reshape(-1, width, width).transpose(1, 0, 2).reshape(width, -1)

    table_rows = action_table.shape[0]
    up_rows = w_up.shape[1]
    ffn = ffn.astype(F32)
    return (
        block_out[:, None],
        grad_input[:, None],
        small[:table_rows],
        small[table_rows : table_rows + 3],
        small[table_rows + 3 : table_rows + 6],
        unblock(main[2048:3584]),
        main[3584:4096],
        unblock(main[:1536]),
        main[1536:2048],
        unblock(ffn[:up_rows]),
        small[table_rows + 6 :].reshape(-1),
        ffn[up_rows:],
    )


def solution(mesh):
    fine = Mesh(mesh.devices.reshape(4, 2, 2, 4, 2), ("x", "zh", "zl", "y", "c"))
    clip = ("zl", "y", "c")
    tokens = P(clip, FRAME_AXES, None, None)
    in_specs = (tokens, P(clip, FRAME_AXES), P(clip)) + (P(),) * 10 + (tokens,)
    out_specs = (tokens, tokens) + (P(),) * 10
    return jax.shard_map(shards, mesh=fine, in_specs=in_specs, out_specs=out_specs, check_vma=False)
```

time: 850 us -> 510 us (0.60)
  waiting for transfers between devices: 466 us -> 124 us
  starting transfers between devices: 0.51 us -> 69.1 us
  blocking collectives: 68 us -> 0 us
  local copies, waits for them, and re-layouts: 108 us -> 126 us
  other arithmetic: 91.3 us -> 75.8 us
  between operations: 14.9 us -> 2.09 us
  matrix products: 92.8 us -> 103 us
    all_gather x1 -> x0, waiting for transfers between devices: 183 us -> none  [shards(): whole = lax.all_gather(kv_local, 'tm', axis=1, tiled=True)]
    reduce_scatter x1 -> x0, waiting for transfers between devices: 155 us -> none  [shards(): lax.psum_scatter(jnp.concatenate([d_key.reshape(row_count, clip_count, pa...]
    psum x1 -> x0, waiting for transfers between devices: 129 us -> none  [shards(): summed = lax.psum(summed, ('tm', 'clip'))]
    all_to_all x0 -> x8, waiting for transfers between devices: none -> 124 us  [the longest x2 52.1 us: reduce_rows(): parts = lax.all_to_all(half.reshape(chips, -1, width), CHIP_AXES, 0, 0)]
    psum x1 -> x0, blocking collectives: 68 us -> none  [shards(): summed = lax.psum(summed, ('tm', 'clip'))]
    all_to_all x0 -> x8, starting transfers between devices: none -> 62.4 us  [the longest x2 18.6 us: reduce_rows(): parts = lax.all_to_all(half.reshape(chips, -1, width), CHIP_AXES, 0, 0)]
    unnamed x142 -> x150, local copies, waits for them, and re-layouts: 51.7 us -> 27.4 us
    convert_element_type x5 -> x12, other arithmetic: 5.07 us -> 28.7 us  [the longest x2 9.4 us: reduce_rows(): half = (mine.astype(F32) + got.astype(F32)).astype(BF)]
  transfers between devices with their start and end apart: 3 -> 12, of which waited for: 3 -> 6; matrix products, arithmetic and copies ran while one was open for 8% -> 30% of each run, Pallas kernels for 0% -> 0%
where the time goes in v1:
time: 510 us; the launch traced here: 501 us
  local copies, waits for them, and re-layouts  126 us (25%)
  waiting for transfers between devices  124 us (24%)
  matrix products  103 us (20%)
  other arithmetic  75.8 us (15%)
  starting transfers between devices  69.1 us (14%)
    all_to_all x2, waiting for transfers between devices, reduce_rows(): parts = lax.all_to_all(half.reshape(chips, -1, width), CHIP_AXES, 0, 0)  52.1 us
    all_to_all x2, waiting for transfers between devices, reduce_rows(): lax.all_to_all(jnp.broadcast_to(part[None], (chips, *part.shape)), CHIP_A...  48.5 us
    unnamed x150, local copies, waits for them, and re-layouts  27.4 us
    dot_general x6, matrix products, mul_t(): lax.dot_general(a, b, (((a.ndim - 1,), (1,)), ((), ())), preferred_elemen...  23.6 us
    dot_general x6, matrix products, mul(): return jnp.dot(a, b, preferred_element_type=F32)  23 us
    dot_general x6, matrix products, wgrad(): lax.dot_general(a, b, (((0,), (0,)), ((), ())), preferred_element_type=F32)  19.9 us
    all_to_all x2, starting transfers between devices, reduce_rows(): parts = lax.all_to_all(half.reshape(chips, -1, width), CHIP_AXES, 0, 0)  18.6 us
    all_to_all x2, starting transfers between devices, reduce_rows(): lax.all_to_all(jnp.broadcast_to(part[None], (chips, *part.shape)), CHIP_A...  16.8 us
  transfers between devices with their start and end apart: 12, of which 6 were waited for; matrix products, arithmetic and copies ran while one was open for 30% of the time, Pallas kernels for 0%

profile of v1, /device:TPU:1, one launch (start us, length us, event | category | flops | bytes accessed | tf_op | source)
XLA Modules:
  0.0 500.9 jit_solution(8200617365951301660)
XLA Ops:
  8.2 3.5 convolution_convert_fusion.1
  11.7 4.6 copy.106
  19.2 6.3 %fusion.135 = (f32[4,8,256]{2,1,0:T(8,128)S(1)}, f32[4,8,256,256]{2,3,1,0:T(8,128)S(1)}) fusion(f32[4,8,256,256]{2,3,1,0:T(8,128)S(1)} %fusion.102), kind=kOutput, calls=%fused_computation.208 | output fusion | flops 8388863 | bytes 16809984 | tf_op jit(solution)/shard_map/sub | solution.py:95
  25.5 3.0 fusion.90
  30.8 8.2 %all-to-all-start = ((bf16[8,4,32,512]{3,2,1,0:T(8,128)(2,1)}), bf16[8,4,32,512]{3,2,1,0:T(8,128)(2,1)S(1)}, u32[]{:S(2)}, u32[]{:S(2)}) async-start(bf16[8,4,32,512]{3,2,1,0:T(8,128)(2,1)} %bitcast.335), calls=%async_computation | async-start | bytes 2097152 | tf_op jit(solution)/shard_map/all_to_all | solution.py:46
  43.6 10.9 %all-to-all-done = bf16[8,4,32,512]{3,2,1,0:T(8,128)(2,1)S(1)} async-done(((bf16[8,4,32,512]{3,2,1,0:T(8,128)(2,1)}), bf16[8,4,32,512]{3,2,1,0:T(8,128)(2,1)S(1)}, u32[]{:S(2)}, u32[]{:S(2)}) %all-to-all-start) | async-done | bytes 1048608 | tf_op jit(solution)/shard_map/all_to_all | solution.py:46
  54.5 4.7 all-to-all-start.2
  61.4 3.5 convolution_convert_fusion
  64.9 8.9 %reshape.451 = bf16[8,4,32,3,8,64]{5,4,3,2,1,0:T(8,128)(2,1)} reshape(bf16[8,4,32,1536]{3,2,1,0:T(8,128)(2,1)} %convolution_convert_fusion) | data formatting | bytes 6291456 | tf_op jit(solution)/shard_map/reshape | solution.py:108
  73.8 3.6 fusion.131
  80.0 16.7 %fusion.136 = (f32[4,32,8,8]{3,2,1,0:T(8,128)S(1)}, f32[4,32,8,8,8]{3,4,2,1,0:T(8,128)S(1)}) fusion(f32[4,32,8,8,8]{3,4,2,1,0:T(8,128)S(1)} %fusion.79, pred[4,8,8]{1,2,0:T(8,128)(4,1)S(1)} %broadcast_and_fusion), kind=kOutput, calls=%fused_computation.209 | output fusion | flops 393223 | bytes 557312 | tf_op jit(solution)/shard_map/sub | solution.py:111
  100.7 4.0 reshape.452
  108.2 7.1 %multiply_convert_fusion.1 = (bf16[8,4,32,2048]{3,2,1,0:T(8,128)(2,1)}, f32[8,4,32,2048]{3,2,1,0:T(8,128)}) fusion(f32[2048]{0:T(1024)S(1)} %copy-done.67, bf16[512,2048]{1,0:T(8,128)(2,1)S(1)} %copy-done, f32[8,4,32,512]{3,2,1,0:T(8,128)S(1)} %get-tuple-element.90, f32[512]{0:T(512)S(1)} %bitcast.368, f32[512]{0:T(512)S(1)} %bitcast.364, ...), kind=kOutput, calls=%fused_computation.19 | convolution fusion | flops 2171076608 | bytes 16797696 | tf_op jit(solution)/shard_map/dot_general | solution.py:29
  115.3 10.6 %convert_reduce_fusion = (f32[2048]{0:T(1024)S(1)}, bf16[8,4,32,2048]{3,2,1,0:T(8,128)(2,1)S(1)}) fusion(f32[8,4,32,2048]{3,2,1,0:T(8,128)} %get-tuple-element.92, f32[2048]{0:T(1024)S(1)} %copy-done.67, bf16[2048,512]{1,0:T(8,128)(2,1)} %param.26, bf16[8,4,32,512]{3,2,1,0:T(8,128)(2,1)} %all-to-all-done.2, f32[8,4]{1,0:T(8,128)S(1)} %fusion.112), kind=kOutput, calls=%fused_computation.16 | convolution fusion | flops 2197288960 | bytes 15745152 | tf_op jit(solution)/shard_map/dot_general | solution.py:33
  125.9 4.1 bitcast_convert_fusion.1
  141.9 5.7 %convert_bitcast_fusion = bf16[8,4,32,8,64]{4,0,3,2,1:T(8,128)(2,1)} fusion(bf16[8,4,32,8,64]{4,3,2,1,0:T(8,128)(2,1)S(1)} %reshape.453, f32[4,32,8,8,8]{3,4,2,1,0:T(8,128)} %copy-done.28, f32[4,32,8,8]{3,2,1,0:T(8,128)} %copy-done.50), kind=kOutput, calls=%fused_computation.108 | convolution fusion | flops 9043968 | bytes 2392064 | tf_op jit(solution)/shard_map/cphfe,fcphd->ecphd/dot_general | solution.py:147
  147.5 3.5 multiply_reduce_fusion.2
  174.4 3.3 reshape.474
  180.4 3.4 fusion.125
  188.4 6.6 %all-to-all-start.3 = ((bf16[8,4,32,512]{3,2,1,0:T(8,128)(2,1)}), bf16[8,4,32,512]{3,2,1,0:T(8,128)(2,1)S(1)}, u32[]{:S(2)}, u32[]{:S(2)}) async-start(bf16[8,4,32,512]{3,2,1,0:T(8,128)(2,1)} %add_convert_fusion), calls=%async_computation.3 | async-start | bytes 2097152 | tf_op jit(solution)/shard_map/all_to_all | solution.py:51
  195.0 5.1 %bitcast_convert_fusion = bf16[2048,512]{1,0:T(8,128)(2,1)S(1)} fusion(bf16[8,4,32,2048]{3,2,1,0:T(8,128)(2,1)} %get-tuple-element.91, bf16[8,4,32,512]{3,2,1,0:T(8,128)(2,1)} %all-to-all-done.2, f32[8,4]{1,0:T(8,128)S(1)} %fusion.112), kind=kOutput, calls=%fused_computation.34 | convolution fusion | flops 2150105088 | bytes 7340160 | tf_op jit(solution)/shard_map/dot_general | solution.py:39
  209.3 4.9 copy.137
  218.6 3.5 fusion.138
  224.7 4.9 fusion.93
  229.7 4.4 multiply_reduce_fusion
  247.5 4.3 fusion.126
  260.1 3.9 fusion.140
  269.2 4.1 fusion.18
  273.4 11.0 %all-to-all-start.6 = ((bf16[64,32,512]{2,1,0:T(8,128)(2,1)}), bf16[64,32,512]{2,1,0:T(8,128)(2,1)}, u32[]{:S(2)}, u32[]{:S(2)}) async-start(bf16[64,32,512]{2,1,0:T(8,128)(2,1)} %bitcast.327), calls=%async_computation.6 | async-start | bytes 4194304 | tf_op jit(solution)/shard_map/all_to_all | solution.py:68
  284.4 5.3 %fusion.17 = bf16[2048,640]{1,0:T(8,128)(2,1)} fusion(s32[]{:T(128)S(6)} %select_n.40, f32[2,2048,512]{2,1,0:T(8,128)} %bitcast.305, f32[2,2048,128]{2,1,0:T(8,128)S(1)} %bitcast.314, bf16[2048,640]{1,0:T(8,128)(2,1)} %collective-permute-done), kind=kLoop, calls=%fused_computation.28 | loop fusion | flops 5242880 | bytes 15728644 | tf_op jit(solution)/shard_map/convert_element_type | solution.py:67
  289.6 22.0 %all-to-all-done.6 = bf16[64,32,512]{2,1,0:T(8,128)(2,1)} async-done(((bf16[64,32,512]{2,1,0:T(8,128)(2,1)}), bf16[64,32,512]{2,1,0:T(8,128)(2,1)}, u32[]{:S(2)}, u32[]{:S(2)}) %all-to-all-start.6) | async-done | bytes 2097184 | tf_op jit(solution)/shard_map/all_to_all | solution.py:68
  311.6 7.6 %all-to-all-start.4 = ((bf16[64,32,640]{2,1,0:T(8,128)(2,1)}), bf16[64,32,640]{2,1,0:T(8,128)(2,1)}, u32[]{:S(2)}, u32[]{:S(2)}) async-start(bf16[64,32,640]{2,1,0:T(8,128)(2,1)} %bitcast.324), calls=%async_computation.4 | async-start | bytes 5242880 | tf_op jit(solution)/shard_map/all_to_all | solution.py:68
  321.1 30.1 %all-to-all-done.4 = bf16[64,32,640]{2,1,0:T(8,128)(2,1)} async-done(((bf16[64,32,640]{2,1,0:T(8,128)(2,1)}), bf16[64,32,640]{2,1,0:T(8,128)(2,1)}, u32[]{:S(2)}, u32[]{:S(2)}) %all-to-all-start.4) | async-done | bytes 2621472 | tf_op jit(solution)/shard_map/all_to_all | solution.py:68
  352.8 9.9 %all-to-all-start.7 = ((bf16[64,32,512]{2,1,0:T(8,128)(2,1)}), bf16[64,32,512]{2,1,0:T(8,128)(2,1)S(1)}, u32[]{:S(2)}, u32[]{:S(2)}) async-start(bf16[64,32,512]{2,1,0:T(8,128)(2,1)} %broadcast_in_dim.40), calls=%async_computation.7 | async-start | bytes 4194304 | tf_op jit(solution)/shard_map/all_to_all | solution.py:70
  364.8 25.4 %all-to-all-done.7 = bf16[64,32,512]{2,1,0:T(8,128)(2,1)S(1)} async-done(((bf16[64,32,512]{2,1,0:T(8,128)(2,1)}), bf16[64,32,512]{2,1,0:T(8,128)(2,1)S(1)}, u32[]{:S(2)}, u32[]{:S(2)}) %all-to-all-start.7) | async-done | bytes 2097184 | tf_op jit(solution)/shard_map/all_to_all | solution.py:70
  393.2 6.9 %all-to-all-start.5 = ((bf16[64,32,640]{2,1,0:T(8,128)(2,1)}), bf16[64,32,640]{2,1,0:T(8,128)(2,1)}, u32[]{:S(2)}, u32[]{:S(2)}) async-start(bf16[64,32,640]{2,1,0:T(8,128)(2,1)} %broadcast_in_dim.39), calls=%async_computation.5 | async-start | bytes 5242880 | tf_op jit(solution)/shard_map/all_to_all | solution.py:70
  402.7 6.2 %add_convert_fusion.1 = bf16[8,4,32,512]{3,2,1,0:T(8,128)(2,1)} fusion(f32[8,4,32,512]{3,2,1,0:T(8,128)S(1)} %copy-done.6, bf16[8,4,32,2048]{3,2,1,0:T(8,128)(2,1)} %get-tuple-element.91, bf16[2048,512]{1,0:T(8,128)(2,1)} %param.26), kind=kOutput, calls=%fused_computation.119 | convolution fusion | flops 2148532224 | bytes 9437184 | tf_op jit(solution)/shard_map/dot_general | solution.py:29
  408.9 23.1 %all-to-all-done.5 = bf16[64,32,640]{2,1,0:T(8,128)(2,1)} async-done(((bf16[64,32,640]{2,1,0:T(8,128)(2,1)}), bf16[64,32,640]{2,1,0:T(8,128)(2,1)}, u32[]{:S(2)}, u32[]{:S(2)}) %all-to-all-start.5) | async-done | bytes 2621472 | tf_op jit(solution)/shard_map/all_to_all | solution.py:70
  432.0 7.6 %all-to-all-start.1 = ((bf16[8,4,32,512]{3,2,1,0:T(8,128)(2,1)}), bf16[8,4,32,512]{3,2,1,0:T(8,128)(2,1)S(1)}, u32[]{:S(2)}, u32[]{:S(2)}) async-start(bf16[8,4,32,512]{3,2,1,0:T(8,128)(2,1)} %add_convert_fusion.1), calls=%async_computation.1 | async-start | bytes 2097152 | tf_op jit(solution)/shard_map/all_to_all | solution.py:51
  441.8 12.8 %all-to-all-done.1 = bf16[8,4,32,512]{3,2,1,0:T(8,128)(2,1)S(1)} async-done(((bf16[8,4,32,512]{3,2,1,0:T(8,128)(2,1)}), bf16[8,4,32,512]{3,2,1,0:T(8,128)(2,1)S(1)}, u32[]{:S(2)}, u32[]{:S(2)}) %all-to-all-start.1) | async-done | bytes 1048608 | tf_op jit(solution)/shard_map/all_to_all | solution.py:51
  464.1 3.0 broadcast_select_fusion.1
  467.1 6.7 %fusion.124 = (f32[4096,640]{1,0:T(8,128)}, bf16[4096,640]{1,0:T(8,128)(2,1)}) fusion(bf16[2048,640]{1,0:T(8,128)(2,1)S(1)} %get-tuple-element.73, bf16[2048,640]{1,0:T(8,128)(2,1)S(1)} %get-tuple-element.72), kind=kLoop, calls=%fused_computation.197 | loop fusion | flops 13107200 | bytes 20971520 | tf_op jit(solution)/shard_map/convert_element_type | solution.py:188
  476.2 3.0 fusion.128
  479.2 6.3 %fusion.129 = (f32[1536,512]{1,0:T(8,128)}, f32[1536,512]{1,0:T(8,128)}) fusion(f32[4096,640]{1,0:T(8,128)} %get-tuple-element.70), kind=kLoop, calls=%fused_computation.202 | loop fusion | bytes 12582912 | tf_op jit(solution)/shard_map/slice | solution.py:206
  486.1 3.6 copy.149
  489.6 3.5 copy.155
  493.2 3.6 copy.148
  496.7 3.7 copy.154
  (256 shorter events, 140.5 us)
Async XLA Ops:
  0.6 107.6 %copy-start = (bf16[512,2048]{1,0:T(8,128)(2,1)S(1)}, bf16[512,2048]{1,0:T(8,128)(2,1)}, u32[]{:S(2)}) copy-start(bf16[512,2048]{1,0:T(8,128)(2,1)} %param.24) | copy-start | bytes 6291460
  0.7 6.0 %copy-start.7 = (bf16[4,1,256,512]{3,2,1,0:T(8,128)(2,1)S(1)}, bf16[4,1,256,512]{3,2,1,0:T(8,128)(2,1)}, u32[]{:S(2)}) copy-start(bf16[4,1,256,512]{3,2,1,0:T(8,128)(2,1)} %param.14) | copy-start | bytes 3145732
  1.6 5.6 %copy-start.60 = (f32[1,512]{1,0:T(1,128)}, f32[1,512]{1,0:T(1,128)S(1)}, u32[]{:S(2)}) copy-start(f32[1,512]{1,0:T(1,128)S(1)} %get-tuple-element.80) | copy-start | bytes 6148
  3.3 25.5 %copy-start.52 = (f32[4,512]{1,0:T(4,128)}, f32[4,512]{1,0:T(4,128)S(1)}, u32[]{:S(2)}) copy-start(f32[4,512]{1,0:T(4,128)S(1)} %fusion.115) | copy-start | bytes 24580
  3.3 4.9 copy-start.64
  4.9 6.8 %copy-start.54 = (f32[4,256]{1,0:T(4,128)}, f32[4,256]{1,0:T(4,128)S(1)}, u32[]{:S(2)}) copy-start(f32[4,256]{1,0:T(4,128)S(1)} %broadcast_multiply_fusion.2) | copy-start | bytes 12292
  6.6 5.1 %copy-start.58 = (f32[4,256]{1,0:T(4,128)}, f32[4,256]{1,0:T(4,128)S(1)}, u32[]{:S(2)}) copy-start(f32[4,256]{1,0:T(4,128)S(1)} %fusion.57) | copy-start | bytes 12292
  6.7 5.0 %copy-start.56 = (f32[4,256]{1,0:T(4,128)}, f32[4,256]{1,0:T(4,128)S(1)}, u32[]{:S(2)}) copy-start(f32[4,256]{1,0:T(4,128)S(1)} %fusion.113) | copy-start | bytes 12292
  25.5 3.4 copy-start.3
  25.5 3.3 copy-start.65
  30.8 23.6 %all-to-all-start = ((bf16[8,4,32,512]{3,2,1,0:T(8,128)(2,1)}), bf16[8,4,32,512]{3,2,1,0:T(8,128)(2,1)S(1)}, u32[]{:S(2)}, u32[]{:S(2)}) async-start(bf16[8,4,32,512]{3,2,1,0:T(8,128)(2,1)} %bitcast.335), calls=%async_computation | async-start | bytes 2097152 | tf_op jit(solution)/shard_map/all_to_all | solution.py:46
  54.5 60.8 %all-to-all-start.2 = ((bf16[8,4,32,512]{3,2,1,0:T(8,128)(2,1)}), bf16[8,4,32,512]{3,2,1,0:T(8,128)(2,1)}, u32[]{:S(2)}, u32[]{:S(2)}) async-start(bf16[8,4,32,512]{3,2,1,0:T(8,128)(2,1)} %bitcast.333), calls=%async_computation.2 | async-start | bytes 2097152 | tf_op jit(solution)/shard_map/all_to_all | solution.py:46
  77.4 19.3 %copy-start.32 = (bf16[8,4,32,1,8,64]{5,4,3,2,1,0:T(8,128)(2,1)}, bf16[8,4,32,1,8,64]{5,4,3,2,1,0:T(8,128)(2,1)S(1)}, u32[]{:S(2)}) copy-start(bf16[8,4,32,1,8,64]{5,4,3,2,1,0:T(8,128)(2,1)S(1)} %get-tuple-element.69) | copy-start | bytes 3145732
  115.3 10.6 %copy-start.5 = (f32[8,4,32,512]{3,2,1,0:T(8,128)S(1)}, f32[8,4,32,512]{3,2,1,0:T(8,128)}, u32[]{:S(2)}) copy-start(f32[8,4,32,512]{3,2,1,0:T(8,128)} %copy-done.4) | copy-start | bytes 6291460
  133.7 3.4 copy-start.49
  141.8 5.7 %copy-start.29 = (f32[4,32,8,8,8]{3,4,2,1,0:T(8,128)S(1)}, f32[4,32,8,8,8]{3,4,2,1,0:T(8,128)}, u32[]{:S(2)}) copy-start(f32[4,32,8,8,8]{3,4,2,1,0:T(8,128)} %copy-done.28) | copy-start | bytes 786436
  141.9 5.7 %copy-start.33 = (bf16[8,4,32,1,8,64]{5,4,3,2,1,0:T(8,128)(2,1)S(1)}, bf16[8,4,32,1,8,64]{5,4,3,2,1,0:T(8,128)(2,1)}, u32[]{:S(2)}) copy-start(bf16[8,4,32,1,8,64]{5,4,3,2,1,0:T(8,128)(2,1)} %copy-done.32) | copy-start | bytes 3145732
  141.9 5.7 %copy-start.51 = (f32[4,32,8,8]{3,2,1,0:T(8,128)S(1)}, f32[4,32,8,8]{3,2,1,0:T(8,128)}, u32[]{:S(2)}) copy-start(f32[4,32,8,8]{3,2,1,0:T(8,128)} %copy-done.50) | copy-start | bytes 98308
  177.8 2.6 copy-start.41
  188.4 33.7 %all-to-all-start.3 = ((bf16[8,4,32,512]{3,2,1,0:T(8,128)(2,1)}), bf16[8,4,32,512]{3,2,1,0:T(8,128)(2,1)S(1)}, u32[]{:S(2)}, u32[]{:S(2)}) async-start(bf16[8,4,32,512]{3,2,1,0:T(8,128)(2,1)} %add_convert_fusion), calls=%async_computation.3 | async-start | bytes 2097152 | tf_op jit(solution)/shard_map/all_to_all | solution.py:51
  195.0 5.1 %copy-start.20 = (bf16[4,512,512]{2,1,0:T(8,128)(2,1)S(1)}, bf16[4,512,512]{2,1,0:T(8,128)(2,1)}, u32[]{:S(2)}) copy-start(bf16[4,512,512]{2,1,0:T(8,128)(2,1)} %copy.150) | copy-start | bytes 6291460
  201.9 3.0 copy-start.17
  209.3 6.7 %copy-start.36 = (bf16[8,4,32,512]{3,2,1,0:T(8,128)(2,1)S(1)}, bf16[8,4,32,512]{3,2,1,0:T(8,128)(2,1)}, u32[]{:S(2)}) copy-start(bf16[8,4,32,512]{3,2,1,0:T(8,128)(2,1)} %copy-done.35) | copy-start | bytes 3145732
  209.3 6.7 %copy-start.40 = (bf16[1024,512]{1,0:T(8,128)(2,1)S(1)}, bf16[1024,512]{1,0:T(8,128)(2,1)}, u32[]{:S(2)}) copy-start(bf16[1024,512]{1,0:T(8,128)(2,1)} %reshape_reshape.10) | copy-start | bytes 3145732
  214.1 55.1 %collective-permute-start.2 = (bf16[2048,512]{1,0:T(8,128)(2,1)}, bf16[2048,512]{1,0:T(8,128)(2,1)}, u32[]{:S(2)}, u32[]{:S(2)}) collective-permute-start(bf16[2048,512]{1,0:T(8,128)(2,1)} %dynamic-slice_bitcast_fusion), channel_id=1, source_target_pairs={{0,1},{1,0},{2,3},{3,2},{4,5},{5,4},{6,7},{7,6},{8,9},{9,8},{10,11... | collective-permute-start | bytes 6291464 | tf_op jit(solution)/shard_map/ppermute | solution.py:56
  216.0 2.5 copy-start.46
  224.7 5.0 copy-start.11
  224.7 9.4 %slice-start = ((s8[8388608]{0:T(1024)(128)(4,1)}), s8[4194304]{0:T(1024)(128)(4,1)S(1)}, s32[]{:S(2)}) async-start(s8[8388608]{0:T(1024)(128)(4,1)} %bitcast.306), calls=%async_computation.8 | async-start | bytes 8388608
  229.7 4.8 slice-start.1
  244.9 2.6 copy-start.8
  245.0 2.6 copy-start.53
  247.5 4.3 copy-start.59
  247.5 4.3 copy-start.57
  260.1 3.9 copy-start.30
  260.1 3.9 copy-start.34
  260.1 3.9 copy-start.37
  265.1 4.1 copy-start.2
  269.2 15.1 %collective-permute-start = (bf16[2048,640]{1,0:T(8,128)(2,1)}, bf16[2048,640]{1,0:T(8,128)(2,1)}, u32[]{:S(2)}, u32[]{:S(2)}) collective-permute-start(bf16[2048,640]{1,0:T(8,128)(2,1)} %fusion.37), channel_id=1, source_target_pairs={{0,1},{1,0},{2,3},{3,2},{4,5},{5,4},{6,7},{7,6},{8,9},{9,8},{10,11... | collective-permute-start | bytes 7864328 | tf_op jit(solution)/shard_map/ppermute | solution.py:56
  273.4 38.3 %all-to-all-start.6 = ((bf16[64,32,512]{2,1,0:T(8,128)(2,1)}), bf16[64,32,512]{2,1,0:T(8,128)(2,1)}, u32[]{:S(2)}, u32[]{:S(2)}) async-start(bf16[64,32,512]{2,1,0:T(8,128)(2,1)} %bitcast.327), calls=%async_computation.6 | async-start | bytes 4194304 | tf_op jit(solution)/shard_map/all_to_all | solution.py:68
  311.6 39.6 %all-to-all-start.4 = ((bf16[64,32,640]{2,1,0:T(8,128)(2,1)}), bf16[64,32,640]{2,1,0:T(8,128)(2,1)}, u32[]{:S(2)}, u32[]{:S(2)}) async-start(bf16[64,32,640]{2,1,0:T(8,128)(2,1)} %bitcast.324), calls=%async_computation.4 | async-start | bytes 5242880 | tf_op jit(solution)/shard_map/all_to_all | solution.py:68
  352.8 37.4 %all-to-all-start.7 = ((bf16[64,32,512]{2,1,0:T(8,128)(2,1)}), bf16[64,32,512]{2,1,0:T(8,128)(2,1)S(1)}, u32[]{:S(2)}, u32[]{:S(2)}) async-start(bf16[64,32,512]{2,1,0:T(8,128)(2,1)} %broadcast_in_dim.40), calls=%async_computation.7 | async-start | bytes 4194304 | tf_op jit(solution)/shard_map/all_to_all | solution.py:70
  393.2 9.5 %copy-start.6 = (f32[8,4,32,512]{3,2,1,0:T(8,128)S(1)}, f32[8,4,32,512]{3,2,1,0:T(8,128)}, u32[]{:S(2)}) copy-start(f32[8,4,32,512]{3,2,1,0:T(8,128)} %copy-done.4) | copy-start | bytes 6291460
  393.2 38.8 %all-to-all-start.5 = ((bf16[64,32,640]{2,1,0:T(8,128)(2,1)}), bf16[64,32,640]{2,1,0:T(8,128)(2,1)}, u32[]{:S(2)}, u32[]{:S(2)}) async-start(bf16[64,32,640]{2,1,0:T(8,128)(2,1)} %broadcast_in_dim.39), calls=%async_computation.5 | async-start | bytes 5242880 | tf_op jit(solution)/shard_map/all_to_all | solution.py:70
  400.1 55.4 %collective-permute-start.3 = (bf16[2048,512]{1,0:T(8,128)(2,1)}, bf16[2048,512]{1,0:T(8,128)(2,1)}, u32[]{:S(2)}, u32[]{:S(2)}) collective-permute-start(bf16[2048,512]{1,0:T(8,128)(2,1)} %bitcast.329), channel_id=1, source_target_pairs={{0,1},{1,0},{2,3},{3,2},{4,5},{5,4},{6,7},{7,6},{8,9},{9,8},{10,11... | collective-permute-start | bytes 6291464 | tf_op jit(solution)/shard_map/ppermute | solution.py:56
  408.9 46.7 %copy-start.19 = (bf16[64,32,512]{2,1,0:T(8,128)(2,1)S(1)}, bf16[64,32,512]{2,1,0:T(8,128)(2,1)}, u32[]{:S(2)}) copy-start(bf16[64,32,512]{2,1,0:T(8,128)(2,1)} %copy-done.18) | copy-start | bytes 6291460
  432.0 22.5 %all-to-all-start.1 = ((bf16[8,4,32,512]{3,2,1,0:T(8,128)(2,1)}), bf16[8,4,32,512]{3,2,1,0:T(8,128)(2,1)S(1)}, u32[]{:S(2)}, u32[]{:S(2)}) async-start(bf16[8,4,32,512]{3,2,1,0:T(8,128)(2,1)} %add_convert_fusion.1), calls=%async_computation.1 | async-start | bytes 2097152 | tf_op jit(solution)/shard_map/all_to_all | solution.py:51
  439.6 24.6 %collective-permute-start.1 = (bf16[2048,640]{1,0:T(8,128)(2,1)}, bf16[2048,640]{1,0:T(8,128)(2,1)}, u32[]{:S(2)}, u32[]{:S(2)}) collective-permute-start(bf16[2048,640]{1,0:T(8,128)(2,1)} %bitcast.79), channel_id=1, source_target_pairs={{0,1},{1,0},{2,3},{3,2},{4,5},{5,4},{6,7},{7,6},{8,9},{9,8},{10,11... | collective-permute-start | bytes 7864328 | tf_op jit(solution)/shard_map/ppermute | solution.py:56
  496.7 3.7 copy-start.1
  (35 other events, 63.0 us)
